TPU v7x, 128 devices: a whole 4x4x4 slice. The times are simulated.
128 devices in a mesh: leaf: 32 (over z, x, core), grp: 4 (over y).
Axes of the slice: x: 4, y: 4, z: 4, core: 2. Of those that a mesh axis runs over, the one named last changes fastest.
Arguments:
- signal: float32 [32, 262144], P(None, ('leaf', 'grp')), may hold values from -6 to 6
- near_index: int32 [1024, 4], P(('leaf', 'grp')), may hold values from 0 to 1023, as said below
- near_block: float32 [1024, 4, 256, 256], P(('leaf', 'grp')), may hold values from -0.1875 to 0.1875
- basis: float32 [1024, 256, 64], P(('leaf', 'grp')), may hold values from -0.375 to 0.375
- far0_index: int32 [1024, 8], P(('leaf', 'grp')), may hold values from 0 to 1023, as said below
- coupling0: float32 [1024, 8, 64, 64], P(('leaf', 'grp')), may hold values from -0.25 to 0.25
- transfer1: float32 [1024, 64, 64], P(('leaf', 'grp')), may hold values from -0.25 to 0.25
- transfer2: float32 [128, 64, 64], P(('leaf', 'grp')), may hold values from -0.375 to 0.375
- far1_index: int32 [128, 8], P(('leaf', 'grp')), may hold values from 0 to 127, as said below
- coupling1: float32 [128, 8, 64, 64], P(('leaf', 'grp')), may hold values from -0.25 to 0.25
- far2_index: int32 [32, 8], P('leaf'), may hold values from 0 to 31, as said below
- coupling2: float32 [32, 8, 64, 64], P('leaf'), may hold values from -0.25 to 0.25
Outputs:
- first_image: float32 [32, 262144], P(None, ('leaf', 'grp'))
- second_image: float32 [32, 262144], P(None, ('leaf', 'grp'))
Inputs may be any that keep to these rules, and one draw needn't show every extreme that they name: `near_index`: row l lists leaves within 8 of l; its first entry is l itself and its second lies at distance exactly 8. `far0_index`: row l lists leaves within 8 of l; its first entry lies at distance exactly 8. `far1_index`: any device clusters; the first column names each device cluster once. `far2_index`: any group clusters; the first column names each group cluster once.
All inputs are finite; a program needn't handle non-finite values.
Results may differ from a plain program's by a relative error of at most 0.000096.
Values sent between devices are 32-bit elements; how exact they have to be, the bound alone decides.
A program may use at most 64 MiB of HBM per device.

v0:
```python
import jax
import jax.numpy as jnp
from jax import lax
from jax.sharding import PartitionSpec as P

HIGHEST_MODE = lax.Precision.HIGHEST


def with_halo(shard, sides, width):
    for axis, dim in sides:
        count, length = (lax.axis_size(axis), shard.shape[dim])
        up = [(i, (i + 1) % count) for i in range(count - 1)]
        down = [(j, i) for i, j in up]
        last = lax.slice_in_dim(shard, length - width, length, axis=dim)
        initial = lax.slice_in_dim(shard, 0, width, axis=dim)
        before = lax.ppermute(last, axis, up)
        after = lax.ppermute(initial, axis, down)
        shard = jnp.concatenate([before, shard, after], axis=dim)
    return shard


def apply_kernel(
    signal,
    near_index,
    near_block,
    basis,
    far0_index,
    coupling0,
    transfer1,
    transfer2,
    far1_index,
    coupling1,
    far2_index,
    coupling2,
):
    rhs_count, columns = signal.shape
    leaf_count, node_count, rank_count = basis.shape
    near_count = near_index.shape[1]
    far_count = far0_index.shape[1]
    fields = signal.reshape(rhs_count, leaf_count, node_count)
    leaf_coefs = jnp.einsum("lnq,sln->slq", basis, fields, precision=HIGHEST_MODE)
    cluster = jnp.einsum("lrq,slr->qs", transfer1, leaf_coefs, precision=HIGHEST_MODE)
    lifted = jnp.dot(transfer2[0].T, cluster, precision=HIGHEST_MODE)
    every_cluster = lax.all_gather(cluster[None], ("leaf", "grp"), axis=0, tiled=True)
    group_coef = lax.psum(lifted, "grp")
    coarse = lax.all_gather(group_coef[None], "leaf", axis=0, tiled=True)
    far_top = jnp.einsum("kqr,krs->qs", coupling2[0], coarse[far2_index[0]], precision=HIGHEST_MODE)
    far_mid = jnp.einsum(
        "kqr,krs->qs", coupling1[0], every_cluster[far1_index[0]], precision=HIGHEST_MODE
    )
    down_mid = jnp.dot(transfer2[0], far_top, precision=HIGHEST_MODE) + far_mid
    offset = lax.axis_index(("leaf", "grp")) * leaf_count - leaf_count
    wide_fields = with_halo(fields, ((("leaf", "grp"), 1),), leaf_count)
    wide_coefs = with_halo(leaf_coefs, ((("leaf", "grp"), 1),), leaf_count)
    far_local = (far0_index - offset).reshape(-1)
    picked = jnp.take(wide_coefs, far_local, axis=1).reshape(
        rhs_count, leaf_count, far_count, rank_count
    )
    far_leaf = jnp.einsum("lkqr,slkr->slq", coupling0, picked, precision=HIGHEST_MODE)
    down_leaf = jnp.einsum("lqr,rs->slq", transfer1, down_mid, precision=HIGHEST_MODE) + far_leaf
    result = jnp.einsum("lnq,slq->sln", basis, down_leaf, precision=HIGHEST_MODE)
    near_local = (near_index - offset).reshape(-1)
    nearby = jnp.take(wide_fields, near_local, axis=1).reshape(
        rhs_count, leaf_count, near_count, node_count
    )
    result = result + jnp.einsum("lkmn,slkn->slm", near_block, nearby, precision=HIGHEST_MODE)
    return result.reshape(rhs_count, columns)


def per_device(
    signal,
    near_index,
    near_block,
    basis,
    far0_index,
    coupling0,
    transfer1,
    transfer2,
    far1_index,
    coupling1,
    far2_index,
    coupling2,
):
    first_image = apply_kernel(
        signal,
        near_index,
        near_block,
        basis,
        far0_index,
        coupling0,
        transfer1,
        transfer2,
        far1_index,
        coupling1,
        far2_index,
        coupling2,
    )
    second_image = apply_kernel(
        first_image,
        near_index,
        near_block,
        basis,
        far0_index,
        coupling0,
        transfer1,
        transfer2,
        far1_index,
        coupling1,
        far2_index,
        coupling2,
    )
    return (first_image, second_image)


def solution(mesh):
    placed = (
        P(None, ("leaf", "grp")),
        P(("leaf", "grp"), None),
        P(("leaf", "grp"), None, None, None),
        P(("leaf", "grp"), None, None),
        P(("leaf", "grp"), None),
        P(("leaf", "grp"), None, None, None),
        P(("leaf", "grp"), None, None),
        P(("leaf", "grp"), None, None),
        P(("leaf", "grp"), None),
        P(("leaf", "grp"), None, None, None),
        P("leaf", None),
        P("leaf", None, None, None),
    )
    return jax.shard_map(
        per_device,
        mesh=mesh,
        in_specs=placed,
        out_specs=(P(None, ("leaf", "grp")), P(None, ("leaf", "grp"))),
        check_vma=False,
    )
```

profile of v0, /device:TPU:1, one launch (start us, length us, event | category | flops | bytes accessed | tf_op | source)
XLA Modules:
  0.0 203.1 jit_solution(199117289005684072)
XLA Ops:
  7.2 1.8 convolution_bitcast_fusion.3
  9.1 6.0 %collective-permute-start.1 = (f32[32,8,64]{2,0,1:T(8,128)S(1)}, f32[32,8,64]{2,0,1:T(8,128)S(1)}, u32[]{:S(2)}, u32[]{:S(2)}) collective-permute-start(f32[32,8,64]{2,0,1:T(8,128)S(1)} %convolution_bitcast_fusion.3), channel_id=1, source_target_pairs={{1,0},{2,1},{3,2},{4,3},{5,4},{6,5},{7,6},{8,7},{9,8},{10,9},{11,1... | collective-permute-start | bytes 196616 | tf_op jit(solution)/shard_map/ppermute | solution.py:17
  15.1 1.9 collective-permute-start
  17.1 1.7 copy.43
  18.7 1.9 collective-permute-start.2
  20.7 4.9 %collective-permute-start.3 = (f32[32,8,256]{2,0,1:T(8,128)}, f32[32,8,256]{2,0,1:T(8,128)}, u32[]{:S(2)}, u32[]{:S(2)}) collective-permute-start(f32[32,8,256]{2,0,1:T(8,128)} %bitcast.138), channel_id=1, source_target_pairs={{1,0},{2,1},{3,2},{4,3},{5,4},{6,5},{7,6},{8,7},{9,8},{10,9},{11,1... | collective-permute-start | bytes 786440 | tf_op jit(solution)/shard_map/ppermute | solution.py:17
  25.5 1.8 fusion.18
  31.8 12.5 %psum.14 = f32[1,64,32]{1,2,0:T(8,128)S(1)} all-reduce(f32[1,64,32]{1,2,0:T(8,128)S(1)} %convolution_bitcast_fusion.7), channel_id=1, replica_groups=mesh['leaf'=32,'grp'=4] {'grp'}, use_global_device_ids=true, to_apply=%region_0.0 | all-reduce | flops 2048 | bytes 16384 | tf_op jit(solution)/shard_map/psum | solution.py:45
  44.3 32.3 %all_gather.12 = f32[32,64,32]{1,2,0:T(8,128)S(1)} all-gather(f32[1,64,32]{1,2,0:T(8,128)S(1)} %psum.14), channel_id=1, replica_groups=mesh['leaf'=32,'grp'=4] {'leaf'}, dimensions={0}, use_global_device_ids=true | all-gather | bytes 270336 | tf_op jit(solution)/shard_map/all_gather | solution.py:46
  82.4 1.7 broadcast_select_fusion.3
  84.1 1.2 pad_maximum_fusion
  85.4 1.7 gather_fusion.5
  87.1 1.4 broadcast_select_fusion.1
  88.5 10.1 %convolution_bitcast_fusion.1 = f32[8,32,256]{2,1,0:T(8,128)S(1)} fusion(f32[32,8,4,256]{3,0,2,1:T(8,128)S(1)} %bitcast.140, f32[8,4,256,256]{3,2,1,0:T(8,128)} %param.18), kind=kOutput, calls=%fused_computation.12 | convolution fusion | flops 805306368 | bytes 9699328 | tf_op jit(solution)/shard_map/lkmn,slkn->slm/dot_general | solution.py:66
  98.6 2.3 %gather_fusion.1 = f32[8,64,32]{1,2,0:T(8,128)S(1)} fusion(f32[128,64,32]{1,2,0:T(8,128)} %all-gather.7.cloned.1.call-done, s32[1024]{0:T(1024)} %pad_clamp_fusion.2), kind=kCustom, calls=%fused_computation.5 | custom fusion | bytes 131104 | tf_op jit(solution)/shard_map/gather | solution.py:49
  103.0 3.2 %fusion.2 = f32[32,8,64]{2,0,1:T(8,128)S(1)} fusion(f32[32,8,64]{2,0,1:T(8,128)S(1)} %fusion.19, f32[32,8,8,64]{3,0,2,1:T(8,128)} %bitcast.142, f32[8,8,64,64]{3,2,1,0:T(8,128)S(1)} %copy-done), kind=kOutput, calls=%fused_computation.18 | convolution fusion | flops 100679680 | bytes 1703936 | tf_op jit(solution)/shard_map/lkqr,slkr->slq/dot_general | solution.py:59
  108.1 2.8 %collective-permute-start.5 = (f32[32,8,64]{2,0,1:T(8,128)S(1)}, f32[32,8,64]{2,0,1:T(8,128)S(1)}, u32[]{:S(2)}, u32[]{:S(2)}) collective-permute-start(f32[32,8,64]{2,0,1:T(8,128)S(1)} %convolution_bitcast_fusion.2), channel_id=1, source_target_pairs={{1,0},{2,1},{3,2},{4,3},{5,4},{6,5},{7,6},{8,7},{9,8},{10,9},{11,1... | collective-permute-start | bytes 196616 | tf_op jit(solution)/shard_map/ppermute | solution.py:17
  110.9 2.4 %collective-permute-start.4 = (f32[32,8,64]{2,0,1:T(8,128)S(1)}, f32[32,8,64]{2,0,1:T(8,128)}, u32[]{:S(2)}, u32[]{:S(2)}) collective-permute-start(f32[32,8,64]{2,0,1:T(8,128)S(1)} %convolution_bitcast_fusion.2), channel_id=1, source_target_pairs={{0,1},{1,2},{2,3},{3,4},{4,5},{5,6},{6,7},{7,8},{8,9},{9,10},{10,1... | collective-permute-start | bytes 196616 | tf_op jit(solution)/shard_map/ppermute | solution.py:16
  113.4 2.3 %collective-permute-start.6 = (f32[32,8,256]{2,0,1:T(8,128)S(1)}, f32[32,8,256]{2,0,1:T(8,128)}, u32[]{:S(2)}, u32[]{:S(2)}) collective-permute-start(f32[32,8,256]{2,0,1:T(8,128)S(1)} %bitcast.143), channel_id=1, source_target_pairs={{0,1},{1,2},{2,3},{3,4},{4,5},{5,6},{6,7},{7,8},{8,9},{9,10},{10,1... | collective-permute-start | bytes 786440 | tf_op jit(solution)/shard_map/ppermute | solution.py:16
  115.7 4.5 %collective-permute-start.7 = (f32[32,8,256]{2,0,1:T(8,128)S(1)}, f32[32,8,256]{2,0,1:T(8,128)}, u32[]{:S(2)}, u32[]{:S(2)}) collective-permute-start(f32[32,8,256]{2,0,1:T(8,128)S(1)} %bitcast.144), channel_id=1, source_target_pairs={{1,0},{2,1},{3,2},{4,3},{5,4},{6,5},{7,6},{8,7},{9,8},{10,9},{11,1... | collective-permute-start | bytes 786440 | tf_op jit(solution)/shard_map/ppermute | solution.py:17
  121.8 14.0 %psum.15 = f32[1,64,32]{1,2,0:T(8,128)S(1)} all-reduce(f32[1,64,32]{1,2,0:T(8,128)S(1)} %convolution_bitcast_fusion.6), channel_id=1, replica_groups=mesh['leaf'=32,'grp'=4] {'grp'}, use_global_device_ids=true, to_apply=%region_1.4 | all-reduce | flops 2048 | bytes 16384 | tf_op jit(solution)/shard_map/psum | solution.py:45
  135.8 29.4 %all_gather.14 = f32[32,64,32]{1,2,0:T(8,128)} all-gather(f32[1,64,32]{1,2,0:T(8,128)S(1)} %psum.15), channel_id=1, replica_groups=mesh['leaf'=32,'grp'=4] {'leaf'}, dimensions={0}, use_global_device_ids=true | all-gather | bytes 270336 | tf_op jit(solution)/shard_map/all_gather | solution.py:46
  165.1 1.7 gather_fusion.2
  166.8 1.3 convolution_bitcast_fusion.9
  169.1 1.7 gather_fusion.6
  170.9 2.4 %broadcast_select_fusion.2 = f32[64,32,64]{2,1,0:T(8,128)} fusion(f32[64,32,64]{2,1,0:T(8,128)} %gather_fusion.6, pred[64]{0:T(512)(128)(4,1)} %compare_and_fusion.1), kind=kLoop, calls=%fused_computation.33 | loop fusion | flops 131072 | bytes 1048640 | tf_op jit(solution)/shard_map/jit(_take)/select_n | solution.py:56
  173.3 1.1 pad_maximum_fusion.1
  174.4 1.7 gather_fusion.7
  176.1 1.4 broadcast_select_fusion
  177.5 10.1 %convolution_bitcast_fusion = f32[8,32,256]{2,1,0:T(8,128)S(1)} fusion(f32[32,8,4,256]{3,0,2,1:T(8,128)S(1)} %bitcast.139, f32[8,4,256,256]{3,2,1,0:T(8,128)} %param.18), kind=kOutput, calls=%fused_computation.11 | convolution fusion | flops 805306368 | bytes 9699328 | tf_op jit(solution)/shard_map/lkmn,slkn->slm/dot_general | solution.py:66
  187.6 2.3 %gather_fusion.3 = f32[8,64,32]{1,2,0:T(8,128)S(1)} fusion(f32[128,64,32]{1,2,0:T(8,128)} %all-gather.9.cloned.1.call-done, s32[1024]{0:T(1024)} %pad_clamp_fusion.2), kind=kCustom, calls=%fused_computation.7 | custom fusion | bytes 131104 | tf_op jit(solution)/shard_map/gather | solution.py:49
  191.9 3.2 %fusion.1 = f32[32,8,64]{2,0,1:T(8,128)S(1)} fusion(f32[32,8,64]{2,0,1:T(8,128)S(1)} %fusion.21, f32[32,8,8,64]{3,0,2,1:T(8,128)} %bitcast.141, f32[8,8,64,64]{3,2,1,0:T(8,128)S(1)} %copy-done), kind=kOutput, calls=%fused_computation.16 | convolution fusion | flops 100679680 | bytes 1703936 | tf_op jit(solution)/shard_map/lkqr,slkr->slq/dot_general | solution.py:59
  (76 shorter events, 20.0 us)
Async XLA Ops:
  7.2 95.8 %copy-start = (f32[8,8,64,64]{3,2,1,0:T(8,128)S(1)}, f32[8,8,64,64]{3,2,1,0:T(8,128)}, u32[]{:S(2)}) copy-start(f32[8,8,64,64]{3,2,1,0:T(8,128)} %param.21) | copy-start | bytes 3145732
  7.2 70.0 %copy-start.6 = (f32[1,8,64,64]{3,2,1,0:T(8,128)S(1)}, f32[1,8,64,64]{3,2,1,0:T(8,128)}, u32[]{:S(2)}) copy-start(f32[1,8,64,64]{3,2,1,0:T(8,128)} %param.27) | copy-start | bytes 393220
  7.2 91.4 %all-gather.7.cloned.1.call-start = ((), (), s32[]{:S(2)}) async-start(), calls=%async_computation | async-start | bytes 2113536 | tf_op jit(solution)/shard_map/all_gather | solution.py:44
  9.1 70.9 %collective-permute-start.1 = (f32[32,8,64]{2,0,1:T(8,128)S(1)}, f32[32,8,64]{2,0,1:T(8,128)S(1)}, u32[]{:S(2)}, u32[]{:S(2)}) collective-permute-start(f32[32,8,64]{2,0,1:T(8,128)S(1)} %convolution_bitcast_fusion.3), channel_id=1, source_target_pairs={{1,0},{2,1},{3,2},{4,3},{5,4},{6,5},{7,6},{8,7},{9,8},{10,9},{11,1... | collective-permute-start | bytes 196616 | tf_op jit(solution)/shard_map/ppermute | solution.py:17
  15.1 65.5 %collective-permute-start = (f32[32,8,64]{2,0,1:T(8,128)S(1)}, f32[32,8,64]{2,0,1:T(8,128)}, u32[]{:S(2)}, u32[]{:S(2)}) collective-permute-start(f32[32,8,64]{2,0,1:T(8,128)S(1)} %convolution_bitcast_fusion.3), channel_id=1, source_target_pairs={{0,1},{1,2},{2,3},{3,4},{4,5},{5,6},{6,7},{7,8},{8,9},{9,10},{10,1... | collective-permute-start | bytes 196616 | tf_op jit(solution)/shard_map/ppermute | solution.py:16
  18.7 65.4 %collective-permute-start.2 = (f32[32,8,256]{2,0,1:T(8,128)}, f32[32,8,256]{2,0,1:T(8,128)}, u32[]{:S(2)}, u32[]{:S(2)}) collective-permute-start(f32[32,8,256]{2,0,1:T(8,128)} %bitcast.138), channel_id=1, source_target_pairs={{0,1},{1,2},{2,3},{3,4},{4,5},{5,6},{6,7},{7,8},{8,9},{9,10},{10,1... | collective-permute-start | bytes 786440 | tf_op jit(solution)/shard_map/ppermute | solution.py:16
  20.7 63.5 %collective-permute-start.3 = (f32[32,8,256]{2,0,1:T(8,128)}, f32[32,8,256]{2,0,1:T(8,128)}, u32[]{:S(2)}, u32[]{:S(2)}) collective-permute-start(f32[32,8,256]{2,0,1:T(8,128)} %bitcast.138), channel_id=1, source_target_pairs={{1,0},{2,1},{3,2},{4,3},{5,4},{6,5},{7,6},{8,7},{9,8},{10,9},{11,1... | collective-permute-start | bytes 786440 | tf_op jit(solution)/shard_map/ppermute | solution.py:17
  27.4 160.2 %all-gather.9.cloned.1.call-start = ((), (), s32[]{:S(2)}) async-start(), calls=%async_computation.1 | async-start | bytes 2113536 | tf_op jit(solution)/shard_map/all_gather | solution.py:44
  30.2 49.7 %copy-start.11 = (s32[1024]{0:T(1024)}, s32[1024]{0:T(1024)S(1)}, u32[]{:S(2)}) copy-start(s32[1024]{0:T(1024)S(1)} %pad_clamp_fusion.3) | copy-start | bytes 12292
  80.0 0.7 copy-start.10
  84.1 2.9 %copy-start.12 = (pred[32]{0:T(512)(128)(4,1)S(1)}, pred[32]{0:T(512)(128)(4,1)}, u32[]{:S(2)}) copy-start(pred[32]{0:T(512)(128)(4,1)} %compare_and_fusion) | copy-start | bytes 100
  88.5 12.4 %copy-start.7 = (f32[1,8,64,64]{3,2,1,0:T(8,128)S(1)}, f32[1,8,64,64]{3,2,1,0:T(8,128)}, u32[]{:S(2)}) copy-start(f32[1,8,64,64]{3,2,1,0:T(8,128)} %param.25) | copy-start | bytes 393220
  88.5 13.7 %copy-start.2 = (f32[8,64,64]{2,1,0:T(8,128)S(1)}, f32[8,64,64]{2,1,0:T(8,128)}, u32[]{:S(2)}) copy-start(f32[8,64,64]{2,1,0:T(8,128)} %param.22) | copy-start | bytes 393220
  100.9 5.3 %copy-start.1 = (f32[8,256,64]{1,2,0:T(8,128)S(1)}, f32[8,256,64]{1,2,0:T(8,128)}, u32[]{:S(2)}) copy-start(f32[8,256,64]{1,2,0:T(8,128)} %param.19) | copy-start | bytes 1572868
  106.2 14.7 %copy-start.9 = (f32[1,64,64]{2,1,0:T(8,128)S(1)}, f32[1,64,64]{2,1,0:T(8,128)}, u32[]{:S(2)}) copy-start(f32[1,64,64]{2,1,0:T(8,128)} %param.23) | copy-start | bytes 49156
  106.6 62.5 %copy-start.4 = (f32[8,32,256]{2,1,0:T(8,128)}, f32[8,32,256]{2,1,0:T(8,128)S(1)}, u32[]{:S(2)}) copy-start(f32[8,32,256]{2,1,0:T(8,128)S(1)} %convolution_add_fusion.1) | copy-start | bytes 786436
  108.1 60.1 %collective-permute-start.5 = (f32[32,8,64]{2,0,1:T(8,128)S(1)}, f32[32,8,64]{2,0,1:T(8,128)S(1)}, u32[]{:S(2)}, u32[]{:S(2)}) collective-permute-start(f32[32,8,64]{2,0,1:T(8,128)S(1)} %convolution_bitcast_fusion.2), channel_id=1, source_target_pairs={{1,0},{2,1},{3,2},{4,3},{5,4},{6,5},{7,6},{8,7},{9,8},{10,9},{11,1... | collective-permute-start | bytes 196616 | tf_op jit(solution)/shard_map/ppermute | solution.py:17
  110.9 57.2 %collective-permute-start.4 = (f32[32,8,64]{2,0,1:T(8,128)S(1)}, f32[32,8,64]{2,0,1:T(8,128)}, u32[]{:S(2)}, u32[]{:S(2)}) collective-permute-start(f32[32,8,64]{2,0,1:T(8,128)S(1)} %convolution_bitcast_fusion.2), channel_id=1, source_target_pairs={{0,1},{1,2},{2,3},{3,4},{4,5},{5,6},{6,7},{7,8},{8,9},{9,10},{10,1... | collective-permute-start | bytes 196616 | tf_op jit(solution)/shard_map/ppermute | solution.py:16
  113.4 59.9 %collective-permute-start.6 = (f32[32,8,256]{2,0,1:T(8,128)S(1)}, f32[32,8,256]{2,0,1:T(8,128)}, u32[]{:S(2)}, u32[]{:S(2)}) collective-permute-start(f32[32,8,256]{2,0,1:T(8,128)S(1)} %bitcast.143), channel_id=1, source_target_pairs={{0,1},{1,2},{2,3},{3,4},{4,5},{5,6},{6,7},{7,8},{8,9},{9,10},{10,1... | collective-permute-start | bytes 786440 | tf_op jit(solution)/shard_map/ppermute | solution.py:16
  115.7 57.5 %collective-permute-start.7 = (f32[32,8,256]{2,0,1:T(8,128)S(1)}, f32[32,8,256]{2,0,1:T(8,128)}, u32[]{:S(2)}, u32[]{:S(2)}) collective-permute-start(f32[32,8,256]{2,0,1:T(8,128)S(1)} %bitcast.144), channel_id=1, source_target_pairs={{1,0},{2,1},{3,2},{4,3},{5,4},{6,5},{7,6},{8,7},{9,8},{10,9},{11,1... | collective-permute-start | bytes 786440 | tf_op jit(solution)/shard_map/ppermute | solution.py:17
  170.9 2.4 %copy-start.5 = (f32[8,32,256]{2,1,0:T(8,128)S(1)}, f32[8,32,256]{2,1,0:T(8,128)}, u32[]{:S(2)}) copy-start(f32[8,32,256]{2,1,0:T(8,128)} %copy-done.4) | copy-start | bytes 786436
  173.2 2.8 %copy-start.13 = (pred[32]{0:T(512)(128)(4,1)S(1)}, pred[32]{0:T(512)(128)(4,1)}, u32[]{:S(2)}) copy-start(pred[32]{0:T(512)(128)(4,1)} %compare_and_fusion) | copy-start | bytes 100
  177.4 12.4 %copy-start.8 = (f32[1,8,64,64]{3,2,1,0:T(8,128)S(1)}, f32[1,8,64,64]{3,2,1,0:T(8,128)}, u32[]{:S(2)}) copy-start(f32[1,8,64,64]{3,2,1,0:T(8,128)} %param.25) | copy-start | bytes 393220
  177.5 13.7 %copy-start.3 = (f32[8,64,64]{2,1,0:T(8,128)S(1)}, f32[8,64,64]{2,1,0:T(8,128)}, u32[]{:S(2)}) copy-start(f32[8,64,64]{2,1,0:T(8,128)} %param.22) | copy-start | bytes 393220
Sparse Core Ops, SparseCore 0:
  27.5 68.0 all-gather.6
  108.2 63.8 all-gather.8
where the time goes:
time: 204 us; the launch traced here: 203 us
  blocking collectives  88.1 us (43%)
  matrix products  39.9 us (20%)
  starting transfers between devices  26.9 us (13%)
  local copies, waits for them, and re-layouts  16.8 us (8%)
  other arithmetic  16.7 us (8%)
  between operations  14.5 us (7%)
    all_gather x2, blocking collectives, apply_kernel(): coarse = lax.all_gather(group_coef[None], 'leaf', axis=0, tiled=True)  61.7 us
    psum x2, blocking collectives, apply_kernel(): group_coef = lax.psum(lifted, 'grp')  26.4 us
    dot_general x2, matrix products, apply_kernel(): jnp.einsum('lkmn,slkn->slm', near_block, nearby, precision=HIGHEST_MODE)  20.1 us
    ppermute x4, starting transfers between devices, with_halo(): after = lax.ppermute(initial, axis, down)  18.2 us
    ppermute x4, starting transfers between devices, with_halo(): before = lax.ppermute(last, axis, up)  8.59 us
    dot_general x2, matrix products, apply_kernel(): jnp.einsum('lkqr,slkr->slq', coupling0, picked, precision=HIGHEST_MODE)  6.31 us
    gather x2, local copies, waits for them, and re-layouts, apply_kernel(): every_cluster[far1_index[0]]  4.54 us
    concatenate x4, other arithmetic, with_halo(): shard = jnp.concatenate([before, shard, after], axis=dim)  4.23 us
  transfers between devices with their start and end apart: 10, of which 0 were waited for; matrix products, arithmetic and copies ran while one was open for 26% of the time, Pallas kernels for 0%

commit v1 on v0

v1 whole, which is shorter than its diff:
```python
import math

import jax
import jax.numpy as jnp
from jax import lax
from jax.experimental import pallas as pl
from jax.experimental.pallas import tpu as pltpu
from jax.sharding import PartitionSpec as P

F32 = jnp.float32
BF16 = jnp.bfloat16
MESH = pl.DeviceIdType.MESH
LEAF = 8
NODE = 256
RANK = 64
RHS = 32
NEAR = 4
FAR = 8
WIDE = RANK * FAR


def dot_nt(a, b):
    return lax.dot_general(a, b, (((1,), (1,)), ((), ())), preferred_element_type=F32)


def dot_nn(a, b):
    return lax.dot_general(a, b, (((1,), (0,)), ((), ())), preferred_element_type=F32)


def dot_full(a, b, dim=1):
    return lax.dot_general(
        a, b, (((dim,), (0,)), ((), ())), precision=lax.Precision.HIGHEST, preferred_element_type=F32
    )


def split(t):
    hi = t.astype(BF16)
    return hi, (t - hi.astype(F32)).astype(BF16)


def stacked(t):
    return jnp.concatenate(split(t), axis=0)


def product(dot, x, wh, wl):
    r = dot(x, wh)
    return r[:RHS] + r[RHS:] + dot(x[:RHS], wl)


def swap(t):
    return pltpu.roll(t, RANK, 1)


def kernel(
    ZN, XN, YN,
    signal, near_index, near_block, basis, far0_index, coupling0, transfer1, transfer2,
    far1_index, coupling1, far2_index, coupling2,
    first, second,
    fld, xs, hf, na, ah, al, bs, t1, t2, c0, c0h, c0l, c1s, c2s, c1f, c1h, c1l, c2f, c2h, c2l,
    yb, cba, cbb, gba, gbb, psx, pbx, psz, pbz, lcs, lch, lcd, acc, ft, si1, si2,
    in_sem, sig_sem, near_sem, out_sem, hs, hr, es, er, ys, yr, zs, zr, gs, gr, fs, fr,
    pxs, pxr, pzs, pzr, k1s, k1r, k2s, k2r, i1s, i1r, i2s, i2r,
):
    leaf = lax.axis_index("leaf")
    y = lax.axis_index("grp")
    c = lax.rem(leaf, 2)
    x = lax.rem(leaf // 2, XN)
    z = leaf // (2 * XN)
    leaves = 2 * XN * ZN
    cb, gb = (cba, cbb), (gba, gbb)
    lane = lax.broadcasted_iota(jnp.int32, (RHS, 2 * RANK), 1)
    low = lane < RANK

    def at(zz, xx, cc, yy):
        return ((zz * XN + xx) * 2 + cc, yy)

    y_peers = [lax.rem(y + o, YN) for o in range(1, YN)]
    x_peers = [lax.rem(x + o, XN) for o in range(1, XN)]
    z_peers = [lax.rem(z + o, ZN) for o in range(1, ZN)]
    sibling = at(z, x, 1 - c, y)
    after = (lax.rem(leaf + (y + 1) // YN, leaves), lax.rem(y + 1, YN))
    before = (lax.rem(leaf + leaves - 1 + (y + YN - 1) // YN, leaves), lax.rem(y + YN - 1, YN))

    def remote(src, dst, ssem, rsem, dev):
        return pltpu.make_async_remote_copy(
            src_ref=src, dst_ref=dst, send_sem=ssem, recv_sem=rsem, device_id=dev, device_id_type=MESH
        )

    loads = []
    for n, (src, dst) in enumerate((
        (coupling1.at[0], c1s), (coupling2.at[0], c2s), (basis, bs), (transfer1, t1), (transfer2.at[0], t2),
        (coupling0, c0), (far1_index, si1.at[x]), (far2_index, si2.at[z]),
    )):
        loads.append(pltpu.make_async_copy(src, dst, in_sem.at[n]))
    for i in range(LEAF):
        pltpu.make_async_copy(signal.at[:, pl.ds(i * NODE, NODE)], fld.at[0, i], sig_sem.at[i]).start()
    for cp in loads:
        cp.start()

    def near_load(l):
        return pltpu.make_async_copy(near_block.at[l], na.at[l], near_sem.at[l])

    for l in range(LEAF):
        near_load(l).start()

    greet = [at(z, x, c, yy) for yy in y_peers] + [at(z, xx, c, y) for xx in x_peers]
    greet += [at(zz, x, c, y) for zz in z_peers] + [sibling, after, before]
    barrier = pltpu.get_barrier_semaphore()
    for dev in greet:
        pl.semaphore_signal(barrier, inc=1, device_id=dev, device_id_type=MESH)
    pl.semaphore_wait(barrier, len(greet))

    def halo(p, side, i):
        return remote(
            fld.at[p, i], hf.at[p, side, i], hs.at[p, side, i], hr.at[p, side, i], after if side == 0 else before
        )

    def send_halo(p):
        for i in range(LEAF):
            halo(p, 0, LEAF - 1 - i).start()
            halo(p, 1, i).start()

    for i in range(LEAF):
        pltpu.make_async_copy(signal.at[:, pl.ds(i * NODE, NODE)], fld.at[0, i], sig_sem.at[i]).wait()
    send_halo(0)

    def coupling_copies():
        out = [
            (remote(c1f.at[x], c1f.at[x], k1s.at[xx], k1r.at[x], at(z, xx, c, y)),
             remote(si1.at[x], si1.at[x], i1s.at[xx], i1r.at[x], at(z, xx, c, y)))
            for xx in x_peers
        ]
        out += [
            (remote(c2f.at[z], c2f.at[z], k2s.at[zz], k2r.at[z], at(zz, x, c, y)),
             remote(si2.at[z], si2.at[z], i2s.at[zz], i2r.at[z], at(zz, x, c, y)))
            for zz in z_peers
        ]
        return out

    for cp in loads:
        cp.wait()
    for j in range(FAR // 2):
        c1f[x, :, pl.ds(2 * j * RANK, 2 * RANK)] = jnp.concatenate([c1s[2 * j], c1s[2 * j + 1]], axis=1)
        c2f[z, :, pl.ds(2 * j * RANK, 2 * RANK)] = jnp.concatenate([c2s[2 * j], c2s[2 * j + 1]], axis=1)
    for pair in coupling_copies():
        for cp in pair:
            cp.start()

    row = lax.broadcasted_iota(jnp.int32, (RANK, 2 * RANK), 0)
    col = lax.broadcasted_iota(jnp.int32, (RANK, 2 * RANK), 1)
    eye = (row == col).astype(F32)

    def fold(l, carry):
        tl = t1[l]
        e = jnp.concatenate([jnp.concatenate([tl, dot_full(tl, t2[...])], axis=1), eye], axis=1)
        hi, lo = split(dot_full(e, bs[l], 0))
        ah[l, NEAR] = hi
        al[l, NEAR] = lo
        xs[LEAF + l] = stacked(fld[0, l])
        ft[l] = jnp.zeros((RHS, NODE), F32)
        xs[l] = jnp.zeros((2 * RHS, NODE), BF16)
        xs[2 * LEAF + l] = jnp.zeros((2 * RHS, NODE), BF16)
        return carry

    lax.fori_loop(0, LEAF, fold, 0)

    base = (leaf * YN + y) * LEAF - LEAF

    def near_split(l, carry):
        near_load(l).wait()
        for k in range(NEAR):
            hi, lo = split(na[l, k])
            ah[l, k] = hi
            al[l, k] = lo
        return carry

    def near_own(l, carry):
        acc[l] = product(dot_nt, xs[LEAF + l], ah[l, 0], al[l, 0])
        return carry

    def coupling_split(l, carry):
        for j in range(FAR // 2):
            hi, lo = split(jnp.concatenate([c0[l, 2 * j], c0[l, 2 * j + 1]], axis=1))
            c0h[l, :, pl.ds(2 * j * RANK, 2 * RANK)] = hi
            c0l[l, :, pl.ds(2 * j * RANK, 2 * RANK)] = lo
        return carry

    def coef_copy(p, side):
        return remote(lcs.at[p], lch.at[p, side], es.at[p, side], er.at[p, side], after if side == 0 else before)

    def y_copy(p, yy):
        return remote(yb.at[p, y], yb.at[p, y], ys.at[p, yy], yr.at[p, y], at(z, x, c, yy))

    def y_wait(p, yy):
        remote(yb.at[p, yy], yb.at[p, yy], ys.at[p, yy], yr.at[p, yy], at(z, x, c, yy)).wait_recv()

    def z_copy(p, zz, slot):
        return remote(cb[p].at[0, slot], cb[p].at[0, slot], zs.at[p, zz], zr.at[p, slot], at(zz, x, c, y))

    def g_copy(p, xx, slot):
        return remote(gb[p].at[0, slot], gb[p].at[0, slot], gs.at[p, xx], gr.at[p, slot], at(z, xx, c, y))

    def forward(p):
        return (
            remote(cb[p].at[0], cb[p].at[1], fs.at[p, 0], fr.at[p, 0], sibling),
            remote(gb[p].at[0], gb[p].at[1], fs.at[p, 1], fr.at[p, 1], sibling),
        )

    def px_copy(p, xx, slot):
        return remote(psx.at[p, xx], pbx.at[p, slot], pxs.at[p, xx], pxr.at[p, slot], at(z, xx, c, y))

    def pz_copy(p, zz, slot):
        return remote(psz.at[p, zz], pbz.at[p, slot], pzs.at[p, zz], pzr.at[p, slot], at(zz, x, c, y))

    def wide(i):
        return jnp.minimum(jnp.maximum(i - base, 0), 3 * LEAF - 1)

    def slot_of(cc):
        return jnp.where(cc == c, 0, 1)

    def mid_tile(p, m, k):
        i = si1[m, 0, k]
        yy = lax.rem(i, YN)
        g = lax.div(i, YN)
        cc = lax.rem(g, 2)
        xx = lax.rem(lax.div(g, 2), XN)
        zz = lax.div(g, 2 * XN)
        t = cb[p][slot_of(cc), zz, lax.div(yy, 2)]
        t = jnp.where(lax.rem(yy, 2) == k % 2, t, swap(t))
        return jnp.where(xx == x, t, 0.0)

    def top_tile(p, m, k):
        i = si2[m, 0, k]
        cc = lax.rem(i, 2)
        xx = lax.rem(lax.div(i, 2), XN)
        zz = lax.div(i, 2 * XN)
        return jnp.where(zz == z, gb[p][slot_of(cc), xx], 0.0)

    def leaf_tile(l, k):
        return lcd[wide(far0_index[l, k])]

    def picked(tile):
        return jnp.concatenate(
            [stacked(jnp.where(low, tile(2 * j), tile(2 * j + 1))) for j in range(FAR // 2)], axis=1
        )

    nothing = jnp.zeros((RHS, RANK), F32)

    def apply(p):
        def up(j, u):
            ra = product(dot_nt, xs[LEAF + 2 * j], ah[2 * j, NEAR], al[2 * j, NEAR])
            rb = product(dot_nt, xs[LEAF + 2 * j + 1], ah[2 * j + 1, NEAR], al[2 * j + 1, NEAR])
            la, lb = ra[:, 2 * RANK:], rb[:, 2 * RANK:]
            lcs[p, j] = la + swap(lb)
            lcd[LEAF + 2 * j] = la + swap(la)
            lcd[LEAF + 2 * j + 1] = lb + swap(lb)
            return u + ra[:, :2 * RANK] + rb[:, :2 * RANK]

        yb[p, y] = lax.fori_loop(0, LEAF // 2, up, jnp.zeros((RHS, 2 * RANK), F32))
        for yy in y_peers:
            y_copy(p, yy).start()
        for side in range(2):
            coef_copy(p, side).start()
        if p == 1:
            send_halo(1)
        else:
            lax.fori_loop(0, LEAF, near_split, 0)
        lax.fori_loop(0, LEAF, near_own, 0)

        for yy in y_peers:
            y_wait(p, yy)
        for j in range(YN // 2):
            cb[p][0, z, j] = jnp.where(low, yb[p, 2 * j], swap(yb[p, 2 * j + 1]))
        total = yb[p, 0]
        for i in range(1, YN):
            total = total + yb[p, i]
        gb[p][0, x] = jnp.where(low, swap(total), total)
        for zz in z_peers:
            z_copy(p, zz, z).start()
        for xx in x_peers:
            g_copy(p, xx, x).start()

        if p == 0:
            lax.fori_loop(0, LEAF, coupling_split, 0)
        for side in range(2):
            coef_copy(p, side).wait_recv()

        def unpack(j, carry):
            for side in range(2):
                t = lch[p, side, j]
                r = swap(t)
                lcd[side * 2 * LEAF + 2 * j] = jnp.where(low, t, r)
                lcd[side * 2 * LEAF + 2 * j + 1] = jnp.where(low, r, t)
            return carry

        lax.fori_loop(0, LEAF // 2, unpack, 0)

        def far_leaf(l, carry):
            v = product(dot_nt, picked(lambda k: leaf_tile(l, k)), c0h[l], c0l[l])
            ft[l, :, pl.ds(2 * RANK, RANK)] = v
            return carry

        lax.fori_loop(0, LEAF, far_leaf, 0)

        for zz in z_peers:
            z_copy(p, zz, zz).wait_recv()
        for xx in x_peers:
            g_copy(p, xx, xx).wait_recv()
        fw = forward(p)
        for cp in fw:
            cp.start()
        if p == 0:
            for xx in x_peers:
                remote(c1f.at[xx], c1f.at[xx], k1s.at[xx], k1r.at[xx], at(z, xx, c, y)).wait_recv()
                remote(si1.at[xx], si1.at[xx], i1s.at[xx], i1r.at[xx], at(z, xx, c, y)).wait_recv()
            for zz in z_peers:
                remote(c2f.at[zz], c2f.at[zz], k2s.at[zz], k2r.at[zz], at(zz, x, c, y)).wait_recv()
                remote(si2.at[zz], si2.at[zz], i2s.at[zz], i2r.at[zz], at(zz, x, c, y)).wait_recv()
            for m in range(XN):
                c1h[m], c1l[m] = split(c1f[m])
            for m in range(ZN):
                c2h[m], c2l[m] = split(c2f[m])
        for cp in fw:
            cp.wait_recv()

        def part_x(m, carry):
            v = product(dot_nt, picked(lambda k: mid_tile(p, m, k)), c1h[m], c1l[m])
            psx[p, m] = jnp.concatenate([v, nothing], axis=1)
            return carry

        def part_z(m, carry):
            v = product(dot_nt, picked(lambda k: top_tile(p, m, k)), c2h[m], c2l[m])
            psz[p, m] = jnp.concatenate([nothing, v], axis=1)
            return carry

        lax.fori_loop(0, XN, part_x, 0)
        for xx in x_peers:
            px_copy(p, xx, x).start()
        lax.fori_loop(0, ZN, part_z, 0)
        for zz in z_peers:
            pz_copy(p, zz, z).start()

        def take(side, i):
            halo(p, side, i).wait_recv()
            xs[side * 2 * LEAF + i] = stacked(hf[p, side, i])

        def near_leaf(l):
            total = acc[l]
            for k in range(1, NEAR):
                total = total + product(dot_nt, xs[wide(near_index[k, l])], ah[l, k], al[l, k])
            acc[l] = total

        half = LEAF // 2

        def take_first(i, carry):
            take(0, LEAF - 1 - i)
            take(1, i)
            return carry

        lax.fori_loop(0, half, take_first, 0)

        def near_pair(j, carry):
            take(0, half - 1 - j)
            take(1, half + j)
            near_leaf(half - 1 - j)
            near_leaf(half + j)
            return carry

        lax.fori_loop(0, half, near_pair, 0)

        for xx in x_peers:
            px_copy(p, xx, xx).wait_recv()
        for zz in z_peers:
            pz_copy(p, zz, zz).wait_recv()
        down = psx[p, x] + psz[p, z]
        for xx in x_peers:
            down = down + pbx[p, xx]
        for zz in z_peers:
            down = down + pbz[p, zz]

        def finish(l, carry):
            ft[l, :, pl.ds(0, 2 * RANK)] = down
            v = acc[l] + product(dot_nn, stacked(ft[l]), ah[l, NEAR], al[l, NEAR])
            fld[p + 1, l] = v
            if p == 0:
                xs[LEAF + l] = stacked(v)
            return carry

        lax.fori_loop(0, LEAF, finish, 0)
        out = first if p == 0 else second
        for l in range(LEAF):
            pltpu.make_async_copy(fld.at[p + 1, l], out.at[:, pl.ds(l * NODE, NODE)], out_sem.at[p, l]).start()

    apply(0)
    apply(1)

    for pair in coupling_copies():
        for cp in pair:
            cp.wait_send()
    for p in range(2):
        for side in range(2):
            for i in range(LEAF):
                halo(p, side, i).wait_send()
            coef_copy(p, side).wait_send()
        for yy in y_peers:
            y_copy(p, yy).wait_send()
        for zz in z_peers:
            z_copy(p, zz, z).wait_send()
            pz_copy(p, zz, z).wait_send()
        for xx in x_peers:
            g_copy(p, xx, x).wait_send()
            px_copy(p, xx, x).wait_send()
        for cp in forward(p):
            cp.wait_send()
        out = first if p == 0 else second
        for l in range(LEAF):
            pltpu.make_async_copy(fld.at[p + 1, l], out.at[:, pl.ds(l * NODE, NODE)], out_sem.at[p, l]).wait()


def solution(mesh):
    leaf, grp = ("leaf", "grp")
    YN = mesh.shape[grp]
    XN = ZN = math.isqrt(mesh.shape[leaf] // 2)
    both = (leaf, grp)
    placed = (
        P(None, both),
        P(both, None),
        P(both, None, None, None),
        P(both, None, None),
        P(both, None),
        P(both, None, None, None),
        P(both, None, None),
        P(both, None, None),
        P(both, None),
        P(both, None, None, None),
        P(leaf, None),
        P(leaf, None, None, None),
    )

    def body(*refs):
        return kernel(ZN, XN, YN, *refs)

    hbm = pl.BlockSpec(memory_space=pl.ANY)
    smem = pl.BlockSpec(memory_space=pltpu.SMEM)
    vmem = pltpu.VMEM
    dma = pltpu.SemaphoreType.DMA
    cols = LEAF * NODE
    scratch = [
        vmem((3, LEAF, RHS, NODE), F32),
        vmem((3 * LEAF, 2 * RHS, NODE), BF16),
        vmem((2, 2, LEAF, RHS, NODE), F32),
        vmem((LEAF, NEAR, NODE, NODE), F32),
        vmem((LEAF, NEAR + 1, NODE, NODE), BF16),
        vmem((LEAF, NEAR + 1, NODE, NODE), BF16),
        vmem((LEAF, RANK, NODE), F32),
        vmem((LEAF, RANK, RANK), F32),
        vmem((RANK, RANK), F32),
        vmem((LEAF, FAR, RANK, RANK), F32),
        vmem((LEAF, RANK, WIDE), BF16),
        vmem((LEAF, RANK, WIDE), BF16),
        vmem((FAR, RANK, RANK), F32),
        vmem((FAR, RANK, RANK), F32),
        vmem((XN, RANK, WIDE), F32),
        vmem((XN, RANK, WIDE), BF16),
        vmem((XN, RANK, WIDE), BF16),
        vmem((ZN, RANK, WIDE), F32),
        vmem((ZN, RANK, WIDE), BF16),
        vmem((ZN, RANK, WIDE), BF16),
        vmem((2, YN, RHS, 2 * RANK), F32),
        vmem((2, ZN, YN // 2, RHS, 2 * RANK), F32),
        vmem((2, ZN, YN // 2, RHS, 2 * RANK), F32),
        vmem((2, XN, RHS, 2 * RANK), F32),
        vmem((2, XN, RHS, 2 * RANK), F32),
        vmem((2, XN, RHS, 2 * RANK), F32),
        vmem((2, XN, RHS, 2 * RANK), F32),
        vmem((2, ZN, RHS, 2 * RANK), F32),
        vmem((2, ZN, RHS, 2 * RANK), F32),
        vmem((2, LEAF // 2, RHS, 2 * RANK), F32),
        vmem((2, 2, LEAF // 2, RHS, 2 * RANK), F32),
        vmem((3 * LEAF, RHS, 2 * RANK), F32),
        vmem((LEAF, RHS, NODE), F32),
        vmem((LEAF, RHS, NODE), F32),
        pltpu.SMEM((XN, 1, FAR), jnp.int32),
        pltpu.SMEM((ZN, 1, FAR), jnp.int32),
        dma((8,)), dma((LEAF,)), dma((LEAF,)), dma((2, LEAF)),
        dma((2, 2, LEAF)), dma((2, 2, LEAF)),
        dma((2, 2)), dma((2, 2)),
        dma((2, YN)), dma((2, YN)),
        dma((2, ZN)), dma((2, ZN)),
        dma((2, XN)), dma((2, XN)),
        dma((2, 2)), dma((2, 2)),
        dma((2, XN)), dma((2, XN)),
        dma((2, ZN)), dma((2, ZN)),
        dma((XN,)), dma((XN,)), dma((ZN,)), dma((ZN,)),
        dma((XN,)), dma((XN,)), dma((ZN,)), dma((ZN,)),
    ]

    def per_device(signal, near_index, near_block, basis, *rest):
        args = (signal, near_index.T, near_block, jnp.swapaxes(basis, 1, 2), *rest)
        call = pl.pallas_call(
            body,
            out_shape=[jax.ShapeDtypeStruct((RHS, cols), F32)] * 2,
            in_specs=[hbm, smem, hbm, hbm, smem] + [hbm] * 7,
            out_specs=[hbm, hbm],
            scratch_shapes=scratch,
            compiler_params=pltpu.CompilerParams(
                collective_id=0, has_side_effects=True, vmem_limit_bytes=56 * 1024 * 1024
            ),
        )
        return tuple(call(*args))

    return jax.shard_map(
        per_device,
        mesh=mesh,
        in_specs=placed,
        out_specs=(P(None, both), P(None, both)),
        check_vma=False,
    )
```

time: 204 us -> 59.3 us (0.29)
  blocking collectives: 88.1 us -> 0 us
  Pallas kernels: 0 us -> 55.1 us
  matrix products: 39.9 us -> 0 us
  starting transfers between devices: 26.9 us -> 0 us
  other arithmetic: 16.7 us -> 0 us
  between operations: 14.5 us -> 0.64 us
  local copies, waits for them, and re-layouts: 16.8 us -> 3.34 us
    all_gather x2 -> x0, blocking collectives: 61.7 us -> none  [apply_kernel(): coarse = lax.all_gather(group_coef[None], 'leaf', axis=0, tiled=True)]
    pallas_call x0 -> x1, Pallas kernels: none -> 55.1 us  [per_device(): return tuple(call(*args))]
    dot_general x20 -> x0, matrix products: 39.9 us -> none  [the longest x2 20.1 us: apply_kernel(): jnp.einsum('lkmn,slkn->slm', near_block, nearby, precision=HIGHEST_MODE)]
    ppermute x8 -> x0, starting transfers between devices: 26.8 us -> none  [the longest x4 18.2 us: with_halo(): after = lax.ppermute(initial, axis, down)]
    psum x2 -> x0, blocking collectives: 26.4 us -> none  [apply_kernel(): group_coef = lax.psum(lifted, 'grp')]
    gather x8 -> x0, local copies, waits for them, and re-layouts: 12.7 us -> none  [the longest x2 4.54 us: apply_kernel(): every_cluster[far1_index[0]]]
    select_n x8 -> x0, other arithmetic: 8.2 us -> none  [the longest x3 4.13 us: apply_kernel(): jnp.take(wide_coefs, far_local, axis=1)]
    concatenate x4 -> x0, other arithmetic: 4.23 us -> none  [with_halo(): shard = jnp.concatenate([before, shard, after], axis=dim)]
  transfers between devices with their start and end apart: 10 -> 0, of which waited for: 0 -> 0; matrix products, arithmetic and copies ran while one was open for 26% -> 0% of each run, Pallas kernels for 0% -> 0%
where the time goes in v1:
time: 59.3 us; the launch traced here: 59.1 us
  Pallas kernels  55.1 us (93%)
  local copies, waits for them, and re-layouts  3.34 us (6%)
  between operations  0.64 us (1%)
    pallas_call x1, Pallas kernels, per_device(): return tuple(call(*args))  55.1 us
    unnamed x2, local copies, waits for them, and re-layouts  3.34 us

profile of v1, /device:TPU:1, one launch (start us, length us, event | category | flops | bytes accessed | tf_op | source)
XLA Modules:
  0.0 59.1 jit_solution(15805740902987560455)
XLA Ops:
  0.6 55.1 %shard_map.131 = (f32[32,2048]{1,0:T(8,128)}, f32[32,2048]{1,0:T(8,128)}) custom-call(f32[32,2048]{1,0:T(8,128)} %refs_0_.1, s32[4,8]{1,0:T(4,128)} %bitcast.3, f32[8,4,256,256]{3,2,1,0:T(8,128)} %refs_2_.1, f32[8,64,256]{2,1,0:T(8,128)} %bitcast.2, s32[8,8]{1,0:T(8,128)} %refs_4_.1, f32[8,8,64,64]{3,2,1,0:T(8,128)} %refs_5_.1, f32[8,64,64]{2,1,0:T(8,128)} %refs_6_.1, ...), custom_call_target="tpu_custom_call" | custom-call | tf_op jit(solution)/shard_map/pallas_call | solution.py:510
  55.7 1.7 %copy.16 = f32[32,2048]{1,0:T(8,128)} copy(f32[32,2048]{1,0:T(8,128)} %get-tuple-element.4) | data formatting | bytes 524288
  57.4 1.7 %copy.17 = f32[32,2048]{1,0:T(8,128)} copy(f32[32,2048]{1,0:T(8,128)} %get-tuple-element.5) | data formatting | bytes 524288

commit v2 on v1

v2 whole, which is shorter than its diff:
```python
import math

import jax
import jax.numpy as jnp
from jax import lax
from jax.experimental import pallas as pl
from jax.experimental.pallas import tpu as pltpu
from jax.sharding import PartitionSpec as P

F32 = jnp.float32
BF16 = jnp.bfloat16
MESH = pl.DeviceIdType.MESH
LEAF = 8
NODE = 256
RANK = 64
RHS = 32
NEAR = 4
FAR = 8
WIDE = RANK * FAR
PACK = RHS // 2
LANES = 2 * RANK


def dot(a, b, da, db):
    return lax.dot_general(a, b, (((da,), (db,)), ((), ())), preferred_element_type=F32)


def dot_nt(a, b):
    return dot(a, b, 1, 1)


def dot_nn(a, b):
    return dot(a, b, 1, 0)


def dot_tn(a, b):
    return dot(a, b, 0, 0)


def split(t):
    hi = t.astype(BF16)
    return hi, (t - hi.astype(F32)).astype(BF16)


def stacked(t):
    return jnp.concatenate(split(t), axis=0)


def product(f, x, wh, wl):
    r = f(x, wh)
    return r[:RHS] + r[RHS:] + f(x[:RHS], wl)


def three(f, a, b):
    return f(a[0], b[0]) + f(a[1], b[0]) + f(a[0], b[1])


def swap(t):
    return pltpu.roll(t, RANK, 1)


def kernel(
    ZN, XN, YN,
    signal, near_hbm, near_block, basis, far0_hbm, coupling0, transfer1, transfer2,
    far1_index, coupling1, far2_index, coupling2,
    first, second,
    fld, xs, hf, na, ah, al, bs, bh, bl, wh, wl, sh, sl, t1, t2, c0, c0h, c0l,
    c1s, c2s, c1f, c1h, c1l, c2f, c2h, c2l,
    yb, cba, cbb, gba, gbb, psx, pbx, psz, pbz, lcs, lch, lcd, acc, near_index, far0_index, si1, si2,
    in_sem, sig_sem, near_sem, out_sem, hs, hr, es, er, ys, yr, zs, zr, gs, gr, fs, fr,
    pxs, pxr, pzs, pzr, k1s, k1r, k2s, k2r, i1s, i1r, i2s, i2r,
):
    leaf = lax.axis_index("leaf")
    y = lax.axis_index("grp")
    c = lax.rem(leaf, 2)
    x = lax.rem(leaf // 2, XN)
    z = leaf // (2 * XN)
    leaves = 2 * XN * ZN
    cb, gb = (cba, cbb), (gba, gbb)
    low = lax.broadcasted_iota(jnp.int32, (RHS, LANES), 1) < RANK
    low_half = lax.broadcasted_iota(jnp.int32, (PACK, LANES), 1) < RANK
    half = LEAF // 2

    def at(zz, xx, cc, yy):
        return ((zz * XN + xx) * 2 + cc, yy)

    y_peers = [lax.rem(y + o, YN) for o in range(1, YN)]
    x_peers = [lax.rem(x + o, XN) for o in range(1, XN)]
    z_peers = [lax.rem(z + o, ZN) for o in range(1, ZN)]
    sibling = at(z, x, 1 - c, y)
    after = (lax.rem(leaf + (y + 1) // YN, leaves), lax.rem(y + 1, YN))
    before = (lax.rem(leaf + leaves - 1 + (y + YN - 1) // YN, leaves), lax.rem(y + YN - 1, YN))

    def remote(src, dst, ssem, rsem, dev):
        return pltpu.make_async_remote_copy(
            src_ref=src, dst_ref=dst, send_sem=ssem, recv_sem=rsem, device_id=dev, device_id_type=MESH
        )

    def pack(v):
        w = jnp.concatenate([v, jnp.zeros_like(v)], axis=1)
        return w[:PACK] + swap(w[PACK:])

    def pack_low(t):
        return jnp.where(low_half, t[:PACK], swap(t[PACK:]))

    def pack_high(t):
        return jnp.where(low_half, swap(t[:PACK]), t[PACK:])

    def pair_of(a, b):
        return jnp.where(
            low, jnp.concatenate([a, swap(a)], axis=0), jnp.concatenate([swap(b), b], axis=0)
        )

    def signal_load(i):
        return pltpu.make_async_copy(signal.at[:, pl.ds(i * NODE, NODE)], fld.at[0, i], sig_sem.at[i])

    def near_load(l):
        return pltpu.make_async_copy(near_block.at[l], na.at[l], near_sem.at[l])

    loads = []
    for n, (src, dst) in enumerate((
        (basis, bs), (transfer1, t1), (transfer2.at[0], t2),
        (far1_index, si1.at[x]), (far2_index, si2.at[z]), (coupling1.at[0], c1s), (coupling2.at[0], c2s),
        (coupling0, c0), (near_hbm, near_index), (far0_hbm, far0_index),
    )):
        loads.append(pltpu.make_async_copy(src, dst, in_sem.at[n]))
    for i in range(LEAF):
        signal_load(i).start()
    for cp in loads:
        cp.start()
    for l in range(LEAF):
        near_load(l).start()

    greet = [at(z, x, c, yy) for yy in y_peers] + [at(z, xx, c, y) for xx in x_peers]
    greet += [at(zz, x, c, y) for zz in z_peers] + [sibling, after, before]
    barrier = pltpu.get_barrier_semaphore()
    for dev in greet:
        pl.semaphore_signal(barrier, inc=1, device_id=dev, device_id_type=MESH)

    def halo(p, side, i):
        return remote(
            fld.at[p, i], hf.at[p, side, i], hs.at[p, side, i], hr.at[p, side, i], after if side == 0 else before
        )

    def send_halo(p):
        for i in range(LEAF):
            halo(p, 0, LEAF - 1 - i).start()
            halo(p, 1, i).start()

    def coupling_copies():
        out = [
            (remote(c1f.at[x], c1f.at[x], k1s.at[xx], k1r.at[x], at(z, xx, c, y)),
             remote(si1.at[x], si1.at[x], i1s.at[xx], i1r.at[x], at(z, xx, c, y)))
            for xx in x_peers
        ]
        out += [
            (remote(c2f.at[z], c2f.at[z], k2s.at[zz], k2r.at[z], at(zz, x, c, y)),
             remote(si2.at[z], si2.at[z], i2s.at[zz], i2r.at[z], at(zz, x, c, y)))
            for zz in z_peers
        ]
        return out

    base = (leaf * YN + y) * LEAF - LEAF

    def near_split(l, carry):
        near_load(l).wait()
        for k in range(NEAR):
            ah[l, k], al[l, k] = split(na[l, k])
        return carry

    def near_own(l, carry):
        acc[l] = product(dot_nt, xs[LEAF + l], ah[l, 0], al[l, 0])
        return carry

    def coupling_split(l, carry):
        for j in range(FAR // 2):
            hi, lo = split(jnp.concatenate([c0[l, 2 * j], c0[l, 2 * j + 1]], axis=1))
            c0h[l, :, pl.ds(j * LANES, LANES)] = hi
            c0l[l, :, pl.ds(j * LANES, LANES)] = lo
        return carry

    def coef_copy(p, side):
        return remote(lcs.at[p], lch.at[p, side], es.at[p, side], er.at[p, side], after if side == 0 else before)

    def y_copy(p, yy, slot):
        return remote(yb.at[p, slot], yb.at[p, slot], ys.at[p, yy], yr.at[p, slot], at(z, x, c, yy))

    def z_copy(p, zz, slot):
        return remote(cb[p].at[0, slot], cb[p].at[0, slot], zs.at[p, zz], zr.at[p, slot], at(zz, x, c, y))

    def g_copy(p, xx, slot):
        return remote(gb[p].at[0, slot], gb[p].at[0, slot], gs.at[p, xx], gr.at[p, slot], at(z, xx, c, y))

    def forward(p):
        return (
            remote(cb[p].at[0], cb[p].at[1], fs.at[p, 0], fr.at[p, 0], sibling),
            remote(gb[p].at[0], gb[p].at[1], fs.at[p, 1], fr.at[p, 1], sibling),
        )

    def px_copy(p, xx, slot):
        return remote(psx.at[p, xx], pbx.at[p, slot], pxs.at[p, xx], pxr.at[p, slot], at(z, xx, c, y))

    def pz_copy(p, zz, slot):
        return remote(psz.at[p, zz], pbz.at[p, slot], pzs.at[p, zz], pzr.at[p, slot], at(zz, x, c, y))

    def wide(i):
        return jnp.minimum(jnp.maximum(i - base, 0), 3 * LEAF - 1)

    def slot_of(cc):
        return jnp.where(cc == c, 0, 1)

    def mid_tile(p, m, k):
        i = si1[m, 0, k]
        g = lax.div(i, YN)
        h = lax.div(g, 2)
        t = cb[p][slot_of(lax.rem(g, 2)), lax.div(h, XN), lax.rem(i, YN)]
        return jnp.where(lax.rem(h, XN) == x, t, 0.0)

    def top_tile(p, m, k):
        i = si2[m, 0, k]
        h = lax.div(i, 2)
        t = gb[p][slot_of(lax.rem(i, 2)), lax.rem(h, XN)]
        return jnp.where(lax.div(h, XN) == z, t, 0.0)

    def leaf_tile(l, k):
        return lcd[wide(far0_index[l, k])]

    def picked(pair):
        return jnp.concatenate([stacked(pair(j)) for j in range(FAR // 2)], axis=1)

    def coefs(p):
        for j in range(half):
            pair = jnp.concatenate(
                [product(dot_nt, xs[LEAF + l], bh[l], bl[l]) for l in (2 * j, 2 * j + 1)], axis=1
            )
            other = swap(pair)
            lcs[p, j] = pair
            lcd[LEAF + 2 * j] = jnp.where(low, pair, other)
            lcd[LEAF + 2 * j + 1] = jnp.where(low, other, pair)

    def send_up(p, u):
        yb[p, y, 0] = pack_low(u)
        yb[p, y, 1] = pack_high(u)
        for yy in y_peers:
            y_copy(p, yy, y).start()

    def group(p):
        for yy in y_peers:
            y_copy(p, yy, yy).wait_recv()
        total = yb[p, 0, 1]
        for i in range(1, YN):
            total = total + yb[p, i, 1]
        gb[p][0, x] = total
        for xx in x_peers:
            g_copy(p, xx, x).start()
        for i in range(YN):
            cb[p][0, z, i] = yb[p, i, 0]
        for zz in z_peers:
            z_copy(p, zz, z).start()

    def far_leaves(p):
        for side in range(2):
            coef_copy(p, side).wait_recv()
        for j in range(half):
            for side in range(2):
                t = lch[p, side, j]
                r = swap(t)
                lcd[side * 2 * LEAF + 2 * j] = jnp.where(low, t, r)
                lcd[side * 2 * LEAF + 2 * j + 1] = jnp.where(low, r, t)

        for l in range(LEAF):
            v = picked(lambda j: jnp.where(low, leaf_tile(l, 2 * j), leaf_tile(l, 2 * j + 1)))
            v = product(dot_nt, v, c0h[l], c0l[l])
            acc[l] += product(dot_nn, stacked(v), bh[l], bl[l])

    def send_forward(p):
        for zz in z_peers:
            z_copy(p, zz, zz).wait_recv()
        for xx in x_peers:
            g_copy(p, xx, xx).wait_recv()
        for cp in forward(p):
            cp.start()

    def partials(p):
        for cp in forward(p):
            cp.wait_recv()
        for m in range(XN):
            v = picked(lambda j: pair_of(mid_tile(p, m, 2 * j), mid_tile(p, m, 2 * j + 1)))
            psx[p, m] = pack(product(dot_nt, v, c1h[m], c1l[m]))
        for xx in x_peers:
            px_copy(p, xx, x).start()
        for m in range(ZN):
            v = picked(lambda j: pair_of(top_tile(p, m, 2 * j), top_tile(p, m, 2 * j + 1)))
            psz[p, m] = pack(product(dot_nt, v, c2h[m], c2l[m]))
        for zz in z_peers:
            pz_copy(p, zz, z).start()

    def near(p):
        def take(side, i):
            halo(p, side, i).wait_recv()
            xs[side * 2 * LEAF + i] = stacked(hf[p, side, i])

        def near_leaf(l):
            total = acc[l]
            for k in range(1, NEAR):
                total = total + product(dot_nt, xs[wide(near_index[k, l])], ah[l, k], al[l, k])
            acc[l] = total

        def take_first(i, carry):
            take(0, LEAF - 1 - i)
            take(1, i)
            return carry

        lax.fori_loop(0, half, take_first, 0)

        def near_pair(j, carry):
            take(0, half - 1 - j)
            take(1, half + j)
            near_leaf(half - 1 - j)
            near_leaf(half + j)
            return carry

        lax.fori_loop(0, half, near_pair, 0)

    def from_above(p):
        for xx in x_peers:
            px_copy(p, xx, xx).wait_recv()
        for zz in z_peers:
            pz_copy(p, zz, zz).wait_recv()
        mid = psx[p, x]
        for xx in x_peers:
            mid = mid + pbx[p, xx]
        top = psz[p, z]
        for zz in z_peers:
            top = top + pbz[p, zz]
        return stacked(pair_of(mid, top))

    def write(p, l):
        out = first if p == 0 else second
        return pltpu.make_async_copy(fld.at[p + 1, l], out.at[:, pl.ds(l * NODE, NODE)], out_sem.at[p, l])

    def finish(p, down):
        for l in range(LEAF):
            v = acc[l] + product(dot_nn, down, wh[l], wl[l])
            fld[p + 1, l] = v
            if p == 0:
                xs[LEAF + l] = stacked(v)
        for l in range(LEAF):
            write(p, l).start()

    for i in range(LEAF):
        signal_load(i).wait()
    for cp in loads[:3]:
        cp.wait()
    for l in range(LEAF):
        bh[l], bl[l] = split(bs[l])
        xs[LEAF + l] = stacked(fld[0, l])
    coefs(0)
    t1p = split(t1[...].reshape(WIDE, RANK))
    t2p = split(t2[...])
    low_level = jnp.concatenate([stacked(lcs[0, j]) for j in range(half)], axis=1)
    cluster = product(dot_nn, low_level, *t1p)
    up = jnp.concatenate([cluster, product(dot_nn, stacked(cluster), *t2p)], axis=1)

    pl.semaphore_wait(barrier, len(greet))
    send_up(0, up)
    for side in range(2):
        coef_copy(0, side).start()
    for cp in loads[3:7]:
        cp.wait()
    for j in range(FAR // 2):
        c1f[x, :, pl.ds(j * LANES, LANES)] = jnp.concatenate([c1s[2 * j], c1s[2 * j + 1]], axis=1)
        c2f[z, :, pl.ds(j * LANES, LANES)] = jnp.concatenate([c2s[2 * j], c2s[2 * j + 1]], axis=1)
    for pair in coupling_copies():
        for cp in pair:
            cp.start()
    send_halo(0)

    for l in range(LEAF):
        xs[l] = jnp.zeros((2 * RHS, NODE), BF16)
        xs[2 * LEAF + l] = jnp.zeros((2 * RHS, NODE), BF16)
    lax.fori_loop(0, LEAF, near_split, 0)
    group(0)

    t1a, t1b = split(t1[...].reshape(WIDE, RANK))
    t12 = three(dot_nn, (t1a, t1b), split(t2[...]))
    for l in range(LEAF):
        e = split(jnp.concatenate([t1[l], t12[l * RANK:(l + 1) * RANK]], axis=1))
        wh[l], wl[l] = split(three(dot_tn, e, (bh[l], bl[l])))
    for cp in loads[7:]:
        cp.wait()
    lax.fori_loop(0, LEAF, coupling_split, 0)
    lax.fori_loop(0, LEAF, near_own, 0)
    send_forward(0)
    square = three(dot_nt, (wh[0], wl[0]), (wh[0], wl[0]))
    for l in range(1, LEAF):
        square = square + three(dot_nt, (wh[l], wl[l]), (wh[l], wl[l]))
    sh[...], sl[...] = split(square)
    far_leaves(0)
    for xx in x_peers:
        remote(c1f.at[xx], c1f.at[xx], k1s.at[xx], k1r.at[xx], at(z, xx, c, y)).wait_recv()
        remote(si1.at[xx], si1.at[xx], i1s.at[xx], i1r.at[xx], at(z, xx, c, y)).wait_recv()
    for zz in z_peers:
        remote(c2f.at[zz], c2f.at[zz], k2s.at[zz], k2r.at[zz], at(zz, x, c, y)).wait_recv()
        remote(si2.at[zz], si2.at[zz], i2s.at[zz], i2r.at[zz], at(zz, x, c, y)).wait_recv()
    for m in range(XN):
        c1h[m], c1l[m] = split(c1f[m])
    for m in range(ZN):
        c2h[m], c2l[m] = split(c2f[m])
    partials(0)
    near(0)
    up = product(dot_nt, stacked(acc[0]), wh[0], wl[0])
    for l in range(1, LEAF):
        up = up + product(dot_nt, stacked(acc[l]), wh[l], wl[l])
    down = from_above(0)

    send_up(1, up + product(dot_nn, down, sh[...], sl[...]))
    finish(0, down)
    coefs(1)
    for side in range(2):
        coef_copy(1, side).start()
    send_halo(1)
    lax.fori_loop(0, LEAF, near_own, 0)
    group(1)
    far_leaves(1)
    send_forward(1)
    partials(1)
    near(1)
    finish(1, from_above(1))

    for pair in coupling_copies():
        for cp in pair:
            cp.wait_send()
    for p in range(2):
        for side in range(2):
            for i in range(LEAF):
                halo(p, side, i).wait_send()
            coef_copy(p, side).wait_send()
        for yy in y_peers:
            y_copy(p, yy, y).wait_send()
        for zz in z_peers:
            z_copy(p, zz, z).wait_send()
            pz_copy(p, zz, z).wait_send()
        for xx in x_peers:
            g_copy(p, xx, x).wait_send()
            px_copy(p, xx, x).wait_send()
        for cp in forward(p):
            cp.wait_send()
        for l in range(LEAF):
            write(p, l).wait()


def hand_over(a, b, first, second, sem):
    copies = [pltpu.make_async_copy(a, first, sem.at[0]), pltpu.make_async_copy(b, second, sem.at[1])]
    for cp in copies:
        cp.start()
    for cp in copies:
        cp.wait()


def solution(mesh):
    leaf, grp = ("leaf", "grp")
    YN = mesh.shape[grp]
    XN = ZN = math.isqrt(mesh.shape[leaf] // 2)
    both = (leaf, grp)
    placed = (
        P(None, both),
        P(both, None),
        P(both, None, None, None),
        P(both, None, None),
        P(both, None),
        P(both, None, None, None),
        P(both, None, None),
        P(both, None, None),
        P(both, None),
        P(both, None, None, None),
        P(leaf, None),
        P(leaf, None, None, None),
    )

    def body(*refs):
        return kernel(ZN, XN, YN, *refs)

    hbm = pl.BlockSpec(memory_space=pl.ANY)
    anywhere = pl.BlockSpec(memory_space=pl.ANY)
    vmem = pltpu.VMEM
    dma = pltpu.SemaphoreType.DMA
    cols = LEAF * NODE
    scratch = [
        vmem((3, LEAF, RHS, NODE), F32),
        vmem((3 * LEAF, 2 * RHS, NODE), BF16),
        vmem((2, 2, LEAF, RHS, NODE), F32),
        vmem((LEAF, NEAR, NODE, NODE), F32),
        vmem((LEAF, NEAR, NODE, NODE), BF16),
        vmem((LEAF, NEAR, NODE, NODE), BF16),
        vmem((LEAF, RANK, NODE), F32),
        vmem((LEAF, RANK, NODE), BF16),
        vmem((LEAF, RANK, NODE), BF16),
        vmem((LEAF, LANES, NODE), BF16),
        vmem((LEAF, LANES, NODE), BF16),
        vmem((LANES, LANES), BF16),
        vmem((LANES, LANES), BF16),
        vmem((LEAF, RANK, RANK), F32),
        vmem((RANK, RANK), F32),
        vmem((LEAF, FAR, RANK, RANK), F32),
        vmem((LEAF, RANK, WIDE), BF16),
        vmem((LEAF, RANK, WIDE), BF16),
        vmem((FAR, RANK, RANK), F32),
        vmem((FAR, RANK, RANK), F32),
        vmem((XN, RANK, WIDE), F32),
        vmem((XN, RANK, WIDE), BF16),
        vmem((XN, RANK, WIDE), BF16),
        vmem((ZN, RANK, WIDE), F32),
        vmem((ZN, RANK, WIDE), BF16),
        vmem((ZN, RANK, WIDE), BF16),
        vmem((2, YN, 2, PACK, LANES), F32),
        vmem((2, ZN, YN, PACK, LANES), F32),
        vmem((2, ZN, YN, PACK, LANES), F32),
        vmem((2, XN, PACK, LANES), F32),
        vmem((2, XN, PACK, LANES), F32),
        vmem((2, XN, PACK, LANES), F32),
        vmem((2, XN, PACK, LANES), F32),
        vmem((2, ZN, PACK, LANES), F32),
        vmem((2, ZN, PACK, LANES), F32),
        vmem((2, LEAF // 2, RHS, 2 * RANK), F32),
        vmem((2, 2, LEAF // 2, RHS, 2 * RANK), F32),
        vmem((3 * LEAF, RHS, 2 * RANK), F32),
        vmem((LEAF, RHS, NODE), F32),
        pltpu.SMEM((NEAR, LEAF), jnp.int32),
        pltpu.SMEM((LEAF, FAR), jnp.int32),
        pltpu.SMEM((XN, 1, FAR), jnp.int32),
        pltpu.SMEM((ZN, 1, FAR), jnp.int32),
        dma((10,)), dma((LEAF,)), dma((LEAF,)), dma((2, LEAF)),
        dma((2, 2, LEAF)), dma((2, 2, LEAF)),
        dma((2, 2)), dma((2, 2)),
        dma((2, YN)), dma((2, YN)),
        dma((2, ZN)), dma((2, ZN)),
        dma((2, XN)), dma((2, XN)),
        dma((2, 2)), dma((2, 2)),
        dma((2, XN)), dma((2, XN)),
        dma((2, ZN)), dma((2, ZN)),
        dma((XN,)), dma((XN,)), dma((ZN,)), dma((ZN,)),
        dma((XN,)), dma((XN,)), dma((ZN,)), dma((ZN,)),
    ]

    def per_device(signal, near_index, near_block, basis, *rest):
        args = (signal, near_index.T, near_block, jnp.swapaxes(basis, 1, 2), *rest)
        call = pl.pallas_call(
            body,
            out_shape=[jax.ShapeDtypeStruct((RHS, cols), F32)] * 2,
            in_specs=[hbm] * 12,
            out_specs=[anywhere, anywhere],
            scratch_shapes=scratch,
            compiler_params=pltpu.CompilerParams(
                collective_id=0, has_side_effects=True, vmem_limit_bytes=56 * 1024 * 1024
            ),
        )
        images = call(*args)
        final = pl.pallas_call(
            hand_over,
            out_shape=[jax.ShapeDtypeStruct((RHS, cols), F32)] * 2,
            in_specs=[pl.BlockSpec(memory_space=vmem)] * 2,
            out_specs=[hbm, hbm],
            scratch_shapes=[dma((2,))],
        )
        return tuple(final(*images))

    return jax.shard_map(
        per_device,
        mesh=mesh,
        in_specs=placed,
        out_specs=(P(None, both), P(None, both)),
        check_vma=False,
    )
```

time: 59.3 us -> 51.3 us (0.87)
  Pallas kernels: 55.1 us -> 50.6 us
  local copies, waits for them, and re-layouts: 3.34 us -> 0 us
    pallas_call x1 -> x2, Pallas kernels: 55.1 us -> 50.6 us  [the longest x1 48.7 us: per_device(): images = call(*args)]
    unnamed x2 -> x0, local copies, waits for them, and re-layouts: 3.34 us -> none
where the time goes in v2:
time: 51.3 us; the launch traced here: 51.2 us
  Pallas kernels  50.6 us (99%)
  between operations  0.64 us (1%)
    pallas_call x1, Pallas kernels, per_device(): images = call(*args)  48.7 us
    pallas_call x1, Pallas kernels, per_device(): return tuple(final(*images))  1.83 us

profile of v2, /device:TPU:1, one launch (start us, length us, event | category | flops | bytes accessed | tf_op | source)
XLA Modules:
  0.0 51.2 jit_solution(15653295477989120598)
XLA Ops:
  0.6 48.7 %shard_map.131 = (f32[32,2048]{1,0:T(8,128)}, f32[32,2048]{1,0:T(8,128)}) custom-call(f32[32,2048]{1,0:T(8,128)} %refs_0_.1, s32[4,8]{1,0:T(4,128)} %bitcast.3, f32[8,4,256,256]{3,2,1,0:T(8,128)} %refs_2_.1, f32[8,64,256]{2,1,0:T(8,128)} %bitcast.2, s32[8,8]{1,0:T(8,128)} %refs_4_.1, f32[8,8,64,64]{3,2,1,0:T(8,128)} %refs_5_.1, f32[8,64,64]{2,1,0:T(8,128)} %refs_6_.1, ...), custom_call_target="tpu_custom_call" | custom-call | tf_op jit(solution)/shard_map/pallas_call | solution.py:558
  49.4 1.8 %shard_map.132 = (f32[32,2048]{1,0:T(8,128)}, f32[32,2048]{1,0:T(8,128)}) custom-call(f32[32,2048]{1,0:T(8,128)} %get-tuple-element.4.a, f32[32,2048]{1,0:T(8,128)} %get-tuple-element.5.b), custom_call_target="tpu_custom_call" | custom-call | tf_op jit(solution)/shard_map/pallas_call | solution.py:566

commit v3 on v2

--- a/solution.py
+++ b/solution.py
@@ -66,8 +66,8 @@
     first, second,
     fld, xs, hf, na, ah, al, bs, bh, bl, wh, wl, sh, sl, t1, t2, c0, c0h, c0l,
     c1s, c2s, c1f, c1h, c1l, c2f, c2h, c2l,
-    yb, cba, cbb, gba, gbb, psx, pbx, psz, pbz, lcs, lch, lcd, acc, near_index, far0_index, si1, si2,
-    in_sem, sig_sem, near_sem, out_sem, hs, hr, es, er, ys, yr, zs, zr, gs, gr, fs, fr,
+    yb, lb, cba, cbb, gba, gbb, psx, pbx, psz, pbz, lcs, lch, lcd, acc, near_index, far0_index, si1, si2,
+    in_sem, sig_sem, near_sem, out_sem, hs, hr, es, er, ys, yr, zs, zr, gs, gr, fs, fr, fgs, fgr,
     pxs, pxr, pzs, pzr, k1s, k1r, k2s, k2r, i1s, i1r, i2s, i2r,
 ):
     leaf = lax.axis_index("leaf")
@@ -131,8 +131,9 @@
     for l in range(LEAF):
         near_load(l).start()
 
-    greet = [at(z, x, c, yy) for yy in y_peers] + [at(z, xx, c, y) for xx in x_peers]
-    greet += [at(zz, x, c, y) for zz in z_peers] + [sibling, after, before]
+    every_y = [lax.rem(y + o, YN) for o in range(YN)]
+    greet = [at(z, x, c, yy) for yy in y_peers] + [at(z, xx, c, yy) for xx in x_peers for yy in every_y]
+    greet += [at(zz, x, c, yy) for zz in z_peers for yy in every_y] + [sibling, after, before]
     barrier = pltpu.get_barrier_semaphore()
     for dev in greet:
         pl.semaphore_signal(barrier, inc=1, device_id=dev, device_id_type=MESH)
@@ -168,9 +169,9 @@
             ah[l, k], al[l, k] = split(na[l, k])
         return carry
 
-    def near_own(l, carry):
-        acc[l] = product(dot_nt, xs[LEAF + l], ah[l, 0], al[l, 0])
-        return carry
+    def near_own():
+        for l in range(LEAF):
+            acc[l] = product(dot_nt, xs[LEAF + l], ah[l, 0], al[l, 0])
 
     def coupling_split(l, carry):
         for j in range(FAR // 2):
@@ -185,17 +186,21 @@
     def y_copy(p, yy, slot):
         return remote(yb.at[p, slot], yb.at[p, slot], ys.at[p, yy], yr.at[p, slot], at(z, x, c, yy))
 
-    def z_copy(p, zz, slot):
-        return remote(cb[p].at[0, slot], cb[p].at[0, slot], zs.at[p, zz], zr.at[p, slot], at(zz, x, c, y))
-
-    def g_copy(p, xx, slot):
-        return remote(gb[p].at[0, slot], gb[p].at[0, slot], gs.at[p, xx], gr.at[p, slot], at(z, xx, c, y))
-
-    def forward(p):
-        return (
-            remote(cb[p].at[0], cb[p].at[1], fs.at[p, 0], fr.at[p, 0], sibling),
-            remote(gb[p].at[0], gb[p].at[1], fs.at[p, 1], fr.at[p, 1], sibling),
-        )
+    def z_copy(p, zz, yy, slot_z, slot_y):
+        return remote(
+            yb.at[p, y, 0], cb[p].at[0, slot_z, slot_y], zs.at[p, zz, yy], zr.at[p, slot_z, slot_y], at(zz, x, c, yy)
+        )
+
+    def g_copy(p, xx, yy, slot_x, slot_y):
+        return remote(
+            yb.at[p, y, 1], lb.at[p, slot_x, slot_y], gs.at[p, xx, yy], gr.at[p, slot_x, slot_y], at(z, xx, c, yy)
+        )
+
+    def forward(p, zz):
+        return remote(cb[p].at[0, zz], cb[p].at[1, zz], fs.at[p, zz], fr.at[p, zz], sibling)
+
+    def forward_top(p):
+        return remote(gb[p].at[0], gb[p].at[1], fgs.at[p], fgr.at[p], sibling)
 
     def px_copy(p, xx, slot):
         return remote(psx.at[p, xx], pbx.at[p, slot], pxs.at[p, xx], pxr.at[p, slot], at(z, xx, c, y))
@@ -241,6 +246,10 @@
     def send_up(p, u):
         yb[p, y, 0] = pack_low(u)
         yb[p, y, 1] = pack_high(u)
+        for xx, zz in zip(x_peers, z_peers):
+            for yy in every_y[1:] + every_y[:1]:
+                g_copy(p, xx, yy, x, y).start()
+                z_copy(p, zz, yy, z, y).start()
         for yy in y_peers:
             y_copy(p, yy, y).start()
 
@@ -251,12 +260,21 @@
         for i in range(1, YN):
             total = total + yb[p, i, 1]
         gb[p][0, x] = total
-        for xx in x_peers:
-            g_copy(p, xx, x).start()
         for i in range(YN):
             cb[p][0, z, i] = yb[p, i, 0]
+        forward(p, z).start()
+        for xx in x_peers:
+            for yy in every_y:
+                g_copy(p, xx, yy, xx, yy).wait_recv()
+            total = lb[p, xx, 0]
+            for i in range(1, YN):
+                total = total + lb[p, xx, i]
+            gb[p][0, xx] = total
+        forward_top(p).start()
         for zz in z_peers:
-            z_copy(p, zz, z).start()
+            for yy in every_y:
+                z_copy(p, zz, yy, zz, yy).wait_recv()
+            forward(p, zz).start()
 
     def far_leaves(p):
         for side in range(2):
@@ -268,22 +286,17 @@
                 lcd[side * 2 * LEAF + 2 * j] = jnp.where(low, t, r)
                 lcd[side * 2 * LEAF + 2 * j + 1] = jnp.where(low, r, t)
 
+        tiles = [
+            picked(lambda j: jnp.where(low, leaf_tile(l, 2 * j), leaf_tile(l, 2 * j + 1))) for l in range(LEAF)
+        ]
+        sums = [stacked(product(dot_nt, tiles[l], c0h[l], c0l[l])) for l in range(LEAF)]
         for l in range(LEAF):
-            v = picked(lambda j: jnp.where(low, leaf_tile(l, 2 * j), leaf_tile(l, 2 * j + 1)))
-            v = product(dot_nt, v, c0h[l], c0l[l])
-            acc[l] += product(dot_nn, stacked(v), bh[l], bl[l])
-
-    def send_forward(p):
-        for zz in z_peers:
-            z_copy(p, zz, zz).wait_recv()
-        for xx in x_peers:
-            g_copy(p, xx, xx).wait_recv()
-        for cp in forward(p):
-            cp.start()
+            acc[l] += product(dot_nn, sums[l], bh[l], bl[l])
 
     def partials(p):
-        for cp in forward(p):
-            cp.wait_recv()
+        for zz in [z] + z_peers:
+            forward(p, zz).wait_recv()
+        forward_top(p).wait_recv()
         for m in range(XN):
             v = picked(lambda j: pair_of(mid_tile(p, m, 2 * j), mid_tile(p, m, 2 * j + 1)))
             psx[p, m] = pack(product(dot_nt, v, c1h[m], c1l[m]))
@@ -390,8 +403,7 @@
     for cp in loads[7:]:
         cp.wait()
     lax.fori_loop(0, LEAF, coupling_split, 0)
-    lax.fori_loop(0, LEAF, near_own, 0)
-    send_forward(0)
+    near_own()
     square = three(dot_nt, (wh[0], wl[0]), (wh[0], wl[0]))
     for l in range(1, LEAF):
         square = square + three(dot_nt, (wh[l], wl[l]), (wh[l], wl[l]))
@@ -420,10 +432,9 @@
     for side in range(2):
         coef_copy(1, side).start()
     send_halo(1)
-    lax.fori_loop(0, LEAF, near_own, 0)
+    near_own()
     group(1)
     far_leaves(1)
-    send_forward(1)
     partials(1)
     near(1)
     finish(1, from_above(1))
@@ -439,13 +450,16 @@
         for yy in y_peers:
             y_copy(p, yy, y).wait_send()
         for zz in z_peers:
-            z_copy(p, zz, z).wait_send()
             pz_copy(p, zz, z).wait_send()
+            for yy in every_y:
+                z_copy(p, zz, yy, z, y).wait_send()
         for xx in x_peers:
-            g_copy(p, xx, x).wait_send()
             px_copy(p, xx, x).wait_send()
-        for cp in forward(p):
-            cp.wait_send()
+            for yy in every_y:
+                g_copy(p, xx, yy, x, y).wait_send()
+        for zz in [z] + z_peers:
+            forward(p, zz).wait_send()
+        forward_top(p).wait_send()
         for l in range(LEAF):
             write(p, l).wait()
 
@@ -514,6 +528,7 @@
         vmem((ZN, RANK, WIDE), BF16),
         vmem((ZN, RANK, WIDE), BF16),
         vmem((2, YN, 2, PACK, LANES), F32),
+        vmem((2, XN, YN, PACK, LANES), F32),
         vmem((2, ZN, YN, PACK, LANES), F32),
         vmem((2, ZN, YN, PACK, LANES), F32),
         vmem((2, XN, PACK, LANES), F32),
@@ -534,9 +549,9 @@
         dma((2, 2, LEAF)), dma((2, 2, LEAF)),
         dma((2, 2)), dma((2, 2)),
         dma((2, YN)), dma((2, YN)),
-        dma((2, ZN)), dma((2, ZN)),
-        dma((2, XN)), dma((2, XN)),
-        dma((2, 2)), dma((2, 2)),
+        dma((2, ZN, YN)), dma((2, ZN, YN)),
+        dma((2, XN, YN)), dma((2, XN, YN)),
+        dma((2, ZN)), dma((2, ZN)), dma((2,)), dma((2,)),
         dma((2, XN)), dma((2, XN)),
         dma((2, ZN)), dma((2, ZN)),
         dma((XN,)), dma((XN,)), dma((ZN,)), dma((ZN,)),

time: 51.3 us -> 47.1 us (0.918)
  Pallas kernels: 50.6 us -> 46.4 us
    pallas_call x1, Pallas kernels: 48.7 us -> 44.5 us  [per_device(): images = call(*args)]
where the time goes in v3:
time: 47.1 us; the launch traced here: 47 us
  Pallas kernels  46.4 us (99%)
  between operations  0.64 us (1%)
    pallas_call x1, Pallas kernels, per_device(): images = call(*args)  44.5 us
    pallas_call x1, Pallas kernels, per_device(): return tuple(final(*images))  1.83 us

profile of v3, /device:TPU:1, one launch (start us, length us, event | category | flops | bytes accessed | tf_op | source)
XLA Modules:
  0.0 47.0 jit_solution(14764325061083739509)
XLA Ops:
  0.6 44.5 %shard_map.131 = (f32[32,2048]{1,0:T(8,128)}, f32[32,2048]{1,0:T(8,128)}) custom-call(f32[32,2048]{1,0:T(8,128)} %refs_0_.1, s32[4,8]{1,0:T(4,128)} %bitcast.3, f32[8,4,256,256]{3,2,1,0:T(8,128)} %refs_2_.1, f32[8,64,256]{2,1,0:T(8,128)} %bitcast.2, s32[8,8]{1,0:T(8,128)} %refs_4_.1, f32[8,8,64,64]{3,2,1,0:T(8,128)} %refs_5_.1, f32[8,64,64]{2,1,0:T(8,128)} %refs_6_.1, ...), custom_call_target="tpu_custom_call" | custom-call | tf_op jit(solution)/shard_map/pallas_call | solution.py:573
  45.2 1.8 %shard_map.132 = (f32[32,2048]{1,0:T(8,128)}, f32[32,2048]{1,0:T(8,128)}) custom-call(f32[32,2048]{1,0:T(8,128)} %get-tuple-element.4.a, f32[32,2048]{1,0:T(8,128)} %get-tuple-element.5.b), custom_call_target="tpu_custom_call" | custom-call | tf_op jit(solution)/shard_map/pallas_call | solution.py:581

commit v4 on v3

--- a/solution.py
+++ b/solution.py
@@ -124,19 +124,23 @@
         (coupling0, c0), (near_hbm, near_index), (far0_hbm, far0_index),
     )):
         loads.append(pltpu.make_async_copy(src, dst, in_sem.at[n]))
+    for cp in loads[:3]:
+        cp.start()
     for i in range(LEAF):
         signal_load(i).start()
-    for cp in loads:
+
+    every_y = [lax.rem(y + o, YN) for o in range(YN)]
+    greet = [at(zz, x, c, yy) for zz in z_peers[1:2] + z_peers[:1] + z_peers[2:] for yy in every_y]
+    greet += [at(z, xx, c, yy) for xx in x_peers[1:2] + x_peers[:1] + x_peers[2:] for yy in every_y]
+    greet += [at(z, x, c, yy) for yy in y_peers] + [sibling, after, before]
+    barrier = pltpu.get_barrier_semaphore()
+    for dev in greet:
+        pl.semaphore_signal(barrier, inc=1, device_id=dev, device_id_type=MESH)
+
+    for cp in loads[3:]:
         cp.start()
     for l in range(LEAF):
         near_load(l).start()
-
-    every_y = [lax.rem(y + o, YN) for o in range(YN)]
-    greet = [at(z, x, c, yy) for yy in y_peers] + [at(z, xx, c, yy) for xx in x_peers for yy in every_y]
-    greet += [at(zz, x, c, yy) for zz in z_peers for yy in every_y] + [sibling, after, before]
-    barrier = pltpu.get_barrier_semaphore()
-    for dev in greet:
-        pl.semaphore_signal(barrier, inc=1, device_id=dev, device_id_type=MESH)
 
     def halo(p, side, i):
         return remote(

time: 47.1 us -> 45.3 us (0.962)
  Pallas kernels: 46.4 us -> 44.5 us
    pallas_call x1, Pallas kernels: 44.5 us -> 42.7 us  [per_device(): images = call(*args)]
where the time goes in v4:
time: 45.3 us; the launch traced here: 45.2 us
  Pallas kernels  44.5 us (98%)
  between operations  0.64 us (1%)
    pallas_call x1, Pallas kernels, per_device(): images = call(*args)  42.7 us
    pallas_call x1, Pallas kernels, per_device(): return tuple(final(*images))  1.83 us

profile of v4, /device:TPU:1, one launch (start us, length us, event | category | flops | bytes accessed | tf_op | source)
XLA Modules:
  0.0 45.2 jit_solution(8080324556192939101)
XLA Ops:
  0.6 42.7 %shard_map.131 = (f32[32,2048]{1,0:T(8,128)}, f32[32,2048]{1,0:T(8,128)}) custom-call(f32[32,2048]{1,0:T(8,128)} %refs_0_.1, s32[4,8]{1,0:T(4,128)} %bitcast.3, f32[8,4,256,256]{3,2,1,0:T(8,128)} %refs_2_.1, f32[8,64,256]{2,1,0:T(8,128)} %bitcast.2, s32[8,8]{1,0:T(8,128)} %refs_4_.1, f32[8,8,64,64]{3,2,1,0:T(8,128)} %refs_5_.1, f32[8,64,64]{2,1,0:T(8,128)} %refs_6_.1, ...), custom_call_target="tpu_custom_call" | custom-call | tf_op jit(solution)/shard_map/pallas_call | solution.py:577
  43.3 1.8 %shard_map.132 = (f32[32,2048]{1,0:T(8,128)}, f32[32,2048]{1,0:T(8,128)}) custom-call(f32[32,2048]{1,0:T(8,128)} %get-tuple-element.4.a, f32[32,2048]{1,0:T(8,128)} %get-tuple-element.5.b), custom_call_target="tpu_custom_call" | custom-call | tf_op jit(solution)/shard_map/pallas_call | solution.py:585

commit v5 on v4

--- a/solution.py
+++ b/solution.py
@@ -137,10 +137,8 @@
     for dev in greet:
         pl.semaphore_signal(barrier, inc=1, device_id=dev, device_id_type=MESH)
 
-    for cp in loads[3:]:
+    for cp in loads[3:7]:
         cp.start()
-    for l in range(LEAF):
-        near_load(l).start()
 
     def halo(p, side, i):
         return remote(
@@ -381,6 +379,10 @@
 
     pl.semaphore_wait(barrier, len(greet))
     send_up(0, up)
+    for l in range(LEAF):
+        near_load(l).start()
+    for cp in loads[7:]:
+        cp.start()
     for side in range(2):
         coef_copy(0, side).start()
     for cp in loads[3:7]:

time: 45.3 us -> 45.3 us (level)
  no operation moved by 1% of the time
where the time goes in v5:
time: 45.3 us; the launch traced here: 45.2 us
  Pallas kernels  44.5 us (98%)
  between operations  0.64 us (1%)
    pallas_call x1, Pallas kernels, per_device(): images = call(*args)  42.7 us
    pallas_call x1, Pallas kernels, per_device(): return tuple(final(*images))  1.83 us

profile of v5, /device:TPU:1, one launch (start us, length us, event | category | flops | bytes accessed | tf_op | source)
XLA Modules:
  0.0 45.2 jit_solution(16522876307754865114)
XLA Ops:
  0.6 42.7 %shard_map.131 = (f32[32,2048]{1,0:T(8,128)}, f32[32,2048]{1,0:T(8,128)}) custom-call(f32[32,2048]{1,0:T(8,128)} %refs_0_.1, s32[4,8]{1,0:T(4,128)} %bitcast.3, f32[8,4,256,256]{3,2,1,0:T(8,128)} %refs_2_.1, f32[8,64,256]{2,1,0:T(8,128)} %bitcast.2, s32[8,8]{1,0:T(8,128)} %refs_4_.1, f32[8,8,64,64]{3,2,1,0:T(8,128)} %refs_5_.1, f32[8,64,64]{2,1,0:T(8,128)} %refs_6_.1, ...), custom_call_target="tpu_custom_call" | custom-call | tf_op jit(solution)/shard_map/pallas_call | solution.py:579
  43.3 1.8 %shard_map.132 = (f32[32,2048]{1,0:T(8,128)}, f32[32,2048]{1,0:T(8,128)}) custom-call(f32[32,2048]{1,0:T(8,128)} %get-tuple-element.4.a, f32[32,2048]{1,0:T(8,128)} %get-tuple-element.5.b), custom_call_target="tpu_custom_call" | custom-call | tf_op jit(solution)/shard_map/pallas_call | solution.py:587
